TPU v7x, 256 devices: a whole 4x4x8 slice. The times are simulated.
256 devices in a mesh: dp: 64 (over z, x, core), mp: 4 (over y).
Axes of the slice: x: 4, y: 4, z: 8, core: 2. Of those that a mesh axis runs over, the one named last changes fastest.
Arguments:
- images: bfloat16 [1024, 64, 1408], P('dp'), may hold values from -8 to 8
- query_states: bfloat16 [1024, 32, 768], P('dp'), may hold values from -6 to 6
- neg_caption: int32 [1024], P('dp'), may hold values from 0 to 1023, as said below
- neg_image: int32 [1024], P('dp'), may hold values from 0 to 1023, as said below
- cross_query: bfloat16 [768, 768], P(None, 'mp'), may hold values from -0.21875 to 0.21875
- cross_kv: bfloat16 [2, 1408, 768], P(None, None, 'mp'), may hold values from -0.15625 to 0.15625
- cross_out: bfloat16 [768, 768], P('mp'), may hold values from -0.21875 to 0.21875
- norm_gain: float32 [768], replicated, may hold values from 0.1 to 1.9
- itm_weight: float32 [768, 2], replicated, may hold values from -1.2 to 1.2
Outputs:
- itm_logits: float32 [3, 1024, 2], P(None, 'dp')
- grad_cross_kv: float32 [2, 1408, 768], P(None, 'dp', 'mp')
Inputs may be any that keep to these rules, and one draw needn't show every extreme that they name: `neg_caption`: among the 16 entries of each aligned block of rows (the rows of one index of dp), at most 2 lie in any one aligned block of 16 pair ids, and some block of pair ids holds exactly 2 entries of every block of rows. No entry equals its own row's pair id. `neg_image`: among the 16 entries of each aligned block of rows (the rows of one index of dp), at most 2 lie in any one aligned block of 16 pair ids, and some block of pair ids holds exactly 2 entries of every block of rows. No entry equals its own row's pair id.
All inputs are finite; a program needn't handle non-finite values.
Results may differ from a plain program's by a relative error of at most 0.011.
Values may be sent and summed in bfloat16 or wider, within the bound.
No kernel may reach another device: no remote copies, remote signals or barrier semaphores. Data moves between devices by JAX's collectives and lax.ppermute only.
A program may use at most 128 MiB of HBM per device.

v0:
```python
import math

import jax
import jax.numpy as jnp
from jax import lax
from jax.sharding import PartitionSpec as P

HEADS = 12


EPS = 1e-06


def plan_slots(partners, pair_count, slot_cap, slot_total):
    owner_block = partners // pair_count
    local_row = partners % pair_count
    row_index = jnp.arange(pair_count, dtype=jnp.int32)
    earlier = (owner_block[:, None] == owner_block[None, :]) & (
        row_index[None, :] < row_index[:, None]
    )
    rank_within = jnp.sum(earlier.astype(jnp.int32), axis=1)
    slot_index = owner_block * slot_cap + rank_within
    chosen = slot_index[:, None] == jnp.arange(slot_total, dtype=jnp.int32)[None, :]
    wanted = jnp.sum(jnp.where(chosen, local_row[:, None], 0), axis=0)
    return (slot_index, chosen.astype(jnp.bfloat16), wanted)


def project(patch_rows, cross_kv):
    return jnp.einsum(
        "npf,kfc->nkpc", patch_rows, cross_kv, preferred_element_type=jnp.float32
    ).astype(jnp.bfloat16)


def split_product(patch_rows, grad_rows):
    upper = grad_rows.astype(jnp.bfloat16)
    lower = (grad_rows - upper.astype(jnp.float32)).astype(jnp.bfloat16)
    first = jnp.einsum("npf,nkpc->kfc", patch_rows, upper, preferred_element_type=jnp.float32)
    return first + jnp.einsum(
        "npf,nkpc->kfc", patch_rows, lower, preferred_element_type=jnp.float32
    )


def norm_forward(residual, gain):
    mean_row = jnp.mean(residual, axis=-1, keepdims=True)
    centred = residual - mean_row
    variance = jnp.mean(centred * centred, axis=-1, keepdims=True)
    inverse = 1.0 / jnp.sqrt(variance + EPS)
    unit_rows = centred * inverse
    return (unit_rows * gain, unit_rows, inverse)


def norm_backward(d_normed, unit_rows, inverse, gain):
    scaled = d_normed * gain
    first = jnp.mean(scaled, axis=-1, keepdims=True)
    second = jnp.mean(scaled * unit_rows, axis=-1, keepdims=True)
    return inverse * (scaled - first - unit_rows * second)


def local(
    images,
    query_states,
    neg_caption,
    neg_image,
    cross_query,
    cross_kv,
    cross_out,
    norm_gain,
    itm_weight,
):
    pair_count = images.shape[0]
    patch_count = images.shape[1]
    vis_width = images.shape[2]
    query_count = query_states.shape[1]
    model_width = query_states.shape[2]
    local_cols = cross_query.shape[1]
    head_size = model_width // HEADS
    heads_local = local_cols // head_size
    score_scale = 1.0 / math.sqrt(head_size)
    groups = lax.axis_size("dp")
    model_groups = lax.axis_size("mp")
    slot_cap = max(2, (2 * pair_count + groups - 1) // groups)
    slot_total = groups * slot_cap
    model_index = lax.axis_index("mp")
    caption_slot, unused_pick, caption_want = plan_slots(
        neg_caption, pair_count, slot_cap, slot_total
    )
    image_slot, image_pick, image_want = plan_slots(neg_image, pair_count, slot_cap, slot_total)
    caption_asked, image_asked = (
        lax.all_to_all(caption_want, "dp", split_axis=0, concat_axis=0, tiled=True),
        lax.all_to_all(image_want, "dp", split_axis=0, concat_axis=0, tiled=True),
    )
    feature_cols = vis_width // model_groups
    image_store = lax.dynamic_slice_in_dim(images, model_index * feature_cols, feature_cols, 2)
    caption_rows, image_rows = (
        lax.all_to_all(
            jnp.take(query_states, caption_asked, axis=0),
            "dp",
            split_axis=0,
            concat_axis=0,
            tiled=True,
        ),
        lax.all_to_all(
            jnp.take(image_store, image_asked, axis=0),
            "dp",
            split_axis=0,
            concat_axis=0,
            tiled=True,
        ),
    )
    neg_states = jnp.take(caption_rows, caption_slot, axis=0)
    neg_part = jnp.take(image_rows, image_slot, axis=0)
    neg_images = lax.all_gather(neg_part, "mp", axis=2, tiled=True)
    both_kv = project(jnp.concatenate([images, neg_images], axis=0), cross_kv)
    own_kv = both_kv[:pair_count]
    neg_kv = both_kv[pair_count:]
    both_states = jnp.concatenate([query_states, neg_states], axis=0)
    query_proj = jnp.dot(both_states, cross_query, preferred_element_type=jnp.float32).astype(
        jnp.bfloat16
    )
    own_query = query_proj[:pair_count]
    neg_query = query_proj[pair_count:]
    example_count = 3 * pair_count
    example_query = jnp.concatenate([own_query, neg_query, own_query], axis=0)
    example_kv = jnp.concatenate([own_kv, own_kv, neg_kv], axis=0)
    example_states = jnp.concatenate([query_states, neg_states, query_states], axis=0)
    query_heads = example_query.reshape(example_count, query_count, heads_local, head_size)
    key_heads = example_kv[:, 0].reshape(example_count, patch_count, heads_local, head_size)
    value_heads = example_kv[:, 1].reshape(example_count, patch_count, heads_local, head_size)
    scores = (
        jnp.einsum("eqhd,ephd->ehqp", query_heads, key_heads, preferred_element_type=jnp.float32)
        * score_scale
    )
    raised = jnp.exp(scores)
    attention = raised / jnp.sum(raised, axis=-1, keepdims=True)
    attention_half = attention.astype(jnp.bfloat16)
    mixed_heads = jnp.einsum(
        "ehqp,ephd->eqhd", attention_half, value_heads, preferred_element_type=jnp.float32
    )
    mixed_heads = mixed_heads.astype(jnp.bfloat16).reshape(example_count, query_count, local_cols)
    partial_value = jnp.dot(mixed_heads, cross_out, preferred_element_type=jnp.float32)
    attended = lax.psum(partial_value.astype(jnp.bfloat16), "mp").astype(jnp.float32)
    residual = example_states.astype(jnp.float32) + attended
    normed, unit_rows, inverse = norm_forward(residual, norm_gain)
    pooled = jnp.mean(normed, axis=1)
    logits = jnp.dot(pooled, itm_weight, precision=lax.Precision.HIGHEST)
    raised_logits = jnp.exp(logits)
    softened = raised_logits / jnp.sum(raised_logits, axis=-1, keepdims=True)
    positive = (jnp.arange(example_count, dtype=jnp.int32) < pair_count).astype(jnp.float32)
    target = jnp.stack([1.0 - positive, positive], axis=-1)
    d_logits = softened - target
    d_pooled = jnp.dot(d_logits, itm_weight.T, precision=lax.Precision.HIGHEST)
    d_normed = jnp.broadcast_to(d_pooled[:, None, :] / query_count, normed.shape)
    d_residual = norm_backward(d_normed, unit_rows, inverse, norm_gain)
    d_res_half = d_residual.astype(jnp.bfloat16)
    d_mixed = jnp.einsum(
        "eqd,cd->eqc", d_res_half, cross_out, preferred_element_type=jnp.float32
    ).astype(jnp.bfloat16)
    d_mixed = d_mixed.reshape(example_count, query_count, heads_local, head_size)
    d_values = jnp.einsum(
        "ehqp,eqhd->ephd", attention_half, d_mixed, preferred_element_type=jnp.float32
    )
    d_attention = jnp.einsum(
        "eqhd,ephd->ehqp", d_mixed, value_heads, preferred_element_type=jnp.float32
    )
    d_scores = (
        attention
        * (d_attention - jnp.sum(d_attention * attention, axis=-1, keepdims=True))
        * score_scale
    )
    d_scores = d_scores.astype(jnp.bfloat16)
    d_keys = jnp.einsum(
        "ehqp,eqhd->ephd", d_scores, query_heads, preferred_element_type=jnp.float32
    )
    d_kv = (
        jnp.stack([d_keys, d_values], axis=1)
        .reshape(example_count, 2, patch_count, local_cols)
        .astype(jnp.bfloat16)
    )
    own_grad = d_kv[:pair_count].astype(jnp.float32) + d_kv[pair_count : 2 * pair_count].astype(
        jnp.float32
    )
    neg_grad = d_kv[2 * pair_count :]
    weight_part = split_product(images, own_grad) + jnp.einsum(
        "npf,nkpc->kfc", neg_images, neg_grad, preferred_element_type=jnp.float32
    )
    grad_part = lax.psum_scatter(weight_part, "dp", scatter_dimension=1, tiled=True)
    return (logits.reshape(3, pair_count, 2), grad_part)


def solution(mesh):
    return jax.shard_map(
        local,
        mesh=mesh,
        in_specs=(
            P("dp", None, None),
            P("dp", None, None),
            P("dp"),
            P("dp"),
            P(None, "mp"),
            P(None, None, "mp"),
            P("mp", None),
            P(),
            P(),
        ),
        out_specs=(P(None, "dp", None), P(None, "dp", "mp")),
        check_vma=False,
    )
```

profile of v0, /device:TPU:2, one launch (start us, length us, event | category | flops | bytes accessed | tf_op | source)
XLA Modules:
  0.0 727.8 jit_solution(1916398014314861231)
XLA Ops:
  9.0 12.0 %all-to-all-start.2 = ((s32[64,2,1]{1,2,0:T(1,128)}), s32[64,2,1]{1,2,0:T(1,128)S(1)}, u32[]{:S(2)}, u32[]{:S(2)}) async-start(s32[64,2,1]{1,2,0:T(1,128)} %bitcast.2), calls=%async_computation.2 | async-start | bytes 65536 | tf_op jit(solution)/shard_map/all_to_all | solution.py:90
  24.3 5.3 all-to-all-done.2
  29.5 5.4 all-to-all-start
  36.5 4.1 gather_fusion.2
  40.6 6.2 broadcast_select_fusion
  46.8 10.7 %all-to-all-start.3 = ((bf16[128,64,352]{2,1,0:T(8,128)(2,1)}), bf16[128,64,352]{2,1,0:T(8,128)(2,1)}, u32[]{:S(2)}, u32[]{:S(2)}) async-start(bf16[128,64,352]{2,1,0:T(8,128)(2,1)} %broadcast_select_fusion), calls=%async_computation.3 | async-start | bytes 12582912 | tf_op jit(solution)/shard_map/all_to_all | solution.py:102
  58.6 3.6 gather_fusion
  62.2 6.1 broadcast_select_fusion.1
  68.3 128.8 %all-to-all-done.3 = bf16[128,64,352]{2,1,0:T(8,128)(2,1)} async-done(((bf16[128,64,352]{2,1,0:T(8,128)(2,1)}), bf16[128,64,352]{2,1,0:T(8,128)(2,1)}, u32[]{:S(2)}, u32[]{:S(2)}) %all-to-all-start.3) | async-done | bytes 5767200 | tf_op jit(solution)/shard_map/all_to_all | solution.py:102
  197.1 7.5 %all-to-all-start.1 = ((bf16[128,32,768]{2,1,0:T(8,128)(2,1)}), bf16[128,32,768]{2,1,0:T(8,128)(2,1)}, u32[]{:S(2)}, u32[]{:S(2)}) async-start(bf16[128,32,768]{2,1,0:T(8,128)(2,1)} %broadcast_select_fusion.1), calls=%async_computation.1 | async-start | bytes 12582912 | tf_op jit(solution)/shard_map/all_to_all | solution.py:95
  204.6 3.5 gather_fusion.3
  210.4 133.7 %all-to-all-done.1 = bf16[128,32,768]{2,1,0:T(8,128)(2,1)} async-done(((bf16[128,32,768]{2,1,0:T(8,128)(2,1)}), bf16[128,32,768]{2,1,0:T(8,128)(2,1)}, u32[]{:S(2)}, u32[]{:S(2)}) %all-to-all-start.1) | async-done | bytes 6291488 | tf_op jit(solution)/shard_map/all_to_all | solution.py:95
  344.1 3.4 gather_fusion.1
  351.3 7.5 %copy.76 = bf16[16,64,1408]{2,1,0:T(8,128)(2,1)} copy(bf16[16,64,1408]{1,0,2:T(8,128)(2,1)} %all-gather.2.cloned.1.call-done) | data formatting | bytes 5767168 | tf_op jit(solution)/shard_map/all_gather | solution.py:112
  358.8 6.1 convert_bitcast_fusion
  367.2 3.9 copy.78
  371.1 4.0 copy.77
  375.1 3.2 fusion.30
  381.9 3.0 reshape.155
  387.5 66.2 %all-reduce.4.cloned.1.call-done = bf16[48,32,768]{2,1,0:T(8,128)(2,1)} async-done(((bf16[48,32,768]{2,1,0:T(8,128)(2,1)}), bf16[48,32,768]{2,1,0:T(8,128)(2,1)}) %all-reduce.4.cloned.1.call-update) | async-done | bytes 2359312 | tf_op jit(solution)/shard_map/psum | solution.py:141
  453.7 2.5 fusion.9
  460.8 3.1 multiply_reduce_fusion
  463.9 3.5 fusion.41
  469.4 3.7 fusion.50
  473.2 2.9 convolution_convert_fusion
  476.1 31.5 %convolution_convert_fusion.1 = bf16[48,3,64,64]{3,2,1,0:T(8,128)(2,1)} fusion(f32[48,3,32,64]{3,2,1,0:T(8,128)} %fusion.50, bf16[48,32,3,64]{3,2,1,0:T(4,128)(2,1)S(1)} %copy-done.8, f32[48,3,32,64]{3,2,1,0:T(8,128)} %copy-done.11, f32[48,3,32]{2,1,0:T(4,128)S(1)} %get-tuple-element.24), kind=kOutput, calls=%fused_computation.51 | convolution fusion | flops 40997440 | bytes 4147200 | tf_op jit(solution)/shard_map/ehqp,eqhd->ephd/dot_general | solution.py:171
  507.6 2.9 copy.87
  510.6 4.1 copy.88
  514.7 3.7 convolution_bitcast_fusion
  520.2 2.8 fusion.20
  523.1 5.5 copy.90
  531.1 188.8 %all-reduce.6.cloned.1.call-done = f32[2,1408,192]{2,0,1:T(2,128)} async-done(((f32[2,1408,192]{2,0,1:T(2,128)}), f32[2,1408,192]{2,0,1:T(2,128)}) %all-reduce.6.cloned.1.call-update) | async-done | bytes 2162704
  (97 shorter events, 33.8 us)
Async XLA Ops:
  7.2 351.6 %copy-start = (bf16[2,1408,192]{1,2,0:T(8,128)(2,1)S(1)}, bf16[2,1408,192]{1,2,0:T(8,128)(2,1)}, u32[]{:S(2)}) copy-start(bf16[2,1408,192]{1,2,0:T(8,128)(2,1)} %param.14) | copy-start | bytes 3244036
  9.0 20.5 %all-to-all-start.2 = ((s32[64,2,1]{1,2,0:T(1,128)}), s32[64,2,1]{1,2,0:T(1,128)S(1)}, u32[]{:S(2)}, u32[]{:S(2)}) async-start(s32[64,2,1]{1,2,0:T(1,128)} %bitcast.2), calls=%async_computation.2 | async-start | bytes 65536 | tf_op jit(solution)/shard_map/all_to_all | solution.py:90
  29.5 17.3 %all-to-all-start = ((s32[64,2,1]{1,2,0:T(1,128)}), s32[64,2,1]{1,2,0:T(1,128)S(1)}, u32[]{:S(2)}, u32[]{:S(2)}) async-start(s32[64,2,1]{1,2,0:T(1,128)} %bitcast), calls=%async_computation | async-start | bytes 65536 | tf_op jit(solution)/shard_map/all_to_all | solution.py:89
  46.8 11.8 %copy-start.2 = (bf16[16,32,768]{2,1,0:T(8,128)(2,1)S(1)}, bf16[16,32,768]{2,1,0:T(8,128)(2,1)}, u32[]{:S(2)}) copy-start(bf16[16,32,768]{2,1,0:T(8,128)(2,1)} %param.10) | copy-start | bytes 2359300
  46.8 150.3 %all-to-all-start.3 = ((bf16[128,64,352]{2,1,0:T(8,128)(2,1)}), bf16[128,64,352]{2,1,0:T(8,128)(2,1)}, u32[]{:S(2)}, u32[]{:S(2)}) async-start(bf16[128,64,352]{2,1,0:T(8,128)(2,1)} %broadcast_select_fusion), calls=%async_computation.3 | async-start | bytes 12582912 | tf_op jit(solution)/shard_map/all_to_all | solution.py:102
  197.1 147.0 %all-to-all-start.1 = ((bf16[128,32,768]{2,1,0:T(8,128)(2,1)}), bf16[128,32,768]{2,1,0:T(8,128)(2,1)}, u32[]{:S(2)}, u32[]{:S(2)}) async-start(bf16[128,32,768]{2,1,0:T(8,128)(2,1)} %broadcast_select_fusion.1), calls=%async_computation.1 | async-start | bytes 12582912 | tf_op jit(solution)/shard_map/all_to_all | solution.py:95
  204.6 146.7 %all-gather.2.cloned.1.call-start = ((), (), s32[]{:S(2)}) async-start(), calls=%async_computation.4 | async-start | bytes 7208960 | tf_op jit(solution)/shard_map/all_gather | solution.py:112
  210.2 243.6 %all-reduce.4.cloned.1.call-start = ((), (), s32[]{:S(2)}) async-start(), calls=%async_computation.5 | async-start | bytes 4718592 | tf_op jit(solution)/shard_map/psum | solution.py:141
  375.1 3.2 copy-start.6
  378.2 1.6 copy-start.11
  379.9 5.0 copy-start.13
  387.2 332.7 %all-reduce.6.cloned.1.call-start = ((), (), s32[]{:S(2)}) async-start(), calls=%async_computation.6 | async-start | bytes 5767168
  453.7 2.5 copy-start.3
  456.2 2.2 copy-start.15
  458.4 1.8 copy-start.14
  467.4 2.0 copy-start.7
  469.4 3.7 copy-start.9
  469.4 3.7 copy-start.12
  473.2 2.9 copy-start.8
  514.7 3.7 copy-start.4
  514.7 3.7 copy-start.5
  518.4 1.8 copy-start.10
  523.1 198.2 %copy-start.1 = (bf16[2,1408,192]{1,2,0:T(8,128)(2,1)S(1)}, bf16[2,1408,192]{1,2,0:T(8,128)(2,1)}, u32[]{:S(2)}) copy-start(bf16[2,1408,192]{1,2,0:T(8,128)(2,1)} %param.14) | copy-start | bytes 3244036
  528.5 0.7 copy-start.16
Sparse Core Ops, SparseCore 0:
  210.3 65.1 all-gather.1
  387.3 66.3 all-reduce.3
  528.7 191.1 all-reduce.5
where the time goes:
time: 729 us; the launch traced here: 728 us
  waiting for transfers between devices  523 us (72%)
  matrix products  65 us (9%)
  local copies, waits for them, and re-layouts  61.2 us (8%)
  starting transfers between devices  36.1 us (5%)
  other arithmetic  27.8 us (4%)
  between operations  14.9 us (2%)
    unnamed x4, waiting for transfers between devices  189 us
    all_to_all x1, waiting for transfers between devices, local(): lax.all_to_all(jnp.take(query_states, caption_asked, axis=0), 'dp', split...  134 us
    all_to_all x1, waiting for transfers between devices, local(): lax.all_to_all(jnp.take(image_store, image_asked, axis=0), 'dp', split_ax...  129 us
    psum x1, waiting for transfers between devices, local(): lax.psum(partial_value.astype(jnp.bfloat16), 'mp').astype(jnp.float32)  66.2 us
    dot_general x1, matrix products, local(): jnp.einsum('ehqp,eqhd->ephd', d_scores, query_heads, preferred_element_ty...  31.5 us
  transfers between devices with their start and end apart: 7, of which 5 were waited for; matrix products, arithmetic and copies ran while one was open for 5% of the time, Pallas kernels for 0%

commit v1 on v0

v1 whole, which is shorter than its diff:
```python
import functools

import jax
import jax.numpy as jnp
from jax import lax
from jax.experimental import pallas as pl
from jax.experimental.pallas import tpu as pltpu
from jax.sharding import PartitionSpec as P

HEADS = 12
EPS = 1e-06
CE = 8
NB = 4
BF16 = jnp.bfloat16
F32 = jnp.float32


def dot(a, b):
    return jnp.dot(a, b, preferred_element_type=F32)


def dot_nt(a, b):
    return lax.dot_general(a, b, (((1,), (1,)), ((), ())), preferred_element_type=F32)


def dot_tn(a, b):
    return lax.dot_general(a, b, (((0,), (0,)), ((), ())), preferred_element_type=F32)


def head_blocks(rows, head):
    lane_head = lax.broadcasted_iota(jnp.int32, rows.shape, 1) // head
    zero = jnp.zeros_like(rows)
    return jnp.concatenate(
        [jnp.where(lane_head == h, rows, zero) for h in range(rows.shape[1] // head)], axis=0
    )


def head_ones(width, head):
    row = lax.broadcasted_iota(jnp.int32, (width, width), 0) // head
    col = lax.broadcasted_iota(jnp.int32, (width, width), 1) // head
    return jnp.where(row == col, 1.0, 0.0).astype(BF16)


def head_sum(values, ones):
    upper = values.astype(BF16)
    lower = (values - upper.astype(F32)).astype(BF16)
    return dot(upper, ones) + dot(lower, ones)


def forward_kernel(
    nch, chunk_img, cap_id, pool, k_ref, v_ref, wq_ref, wot_ref, gain_ref, itm_ref,
    q_out, p_out, d_out, log_out, xbuf, sems, *, head, scale,
):
    step = pl.program_id(0)
    shards, _, cols = k_ref.shape
    patches = head
    slots = NB * CE
    blocks = (nch[0] + NB - 1) // NB

    def fetch(blk):
        def one(j, carry):
            slot = blk * slots + j
            pltpu.make_async_copy(pool.at[cap_id[slot]], xbuf.at[slot], sems.at[blk]).start()
            return carry

        lax.fori_loop(0, slots, one, 0)

    @pl.when(step == 0)
    def _():
        def each(blk, carry):
            fetch(blk)
            return carry

        lax.fori_loop(0, blocks, each, 0)

    @pl.when(step < blocks)
    def _():
        first = pl.multiple_of(step * slots, slots)
        mine = xbuf.at[pl.ds(first, slots)]
        pltpu.make_async_copy(pool.at[pl.ds(0, slots)], mine, sems.at[step]).wait()
        x16 = mine[...].astype(F32)
        rows = x16.shape[1] // 2
        xf = jnp.concatenate([x16[:, :rows], x16[:, rows:]], axis=-1)
        width = xf.shape[-1]
        xf = xf.reshape(slots * rows, width)
        xb = xf.astype(BF16)
        ones = head_ones(cols, head)
        attended = jnp.zeros_like(xf)
        crow = CE * rows
        for s in range(shards):
            q = dot(xb, wq_ref[s]).astype(BF16)
            q_out[s] = q
            scores = []
            for c in range(NB):
                img = chunk_img[step * NB + c]
                at = pl.multiple_of(img * patches, patches)
                kbd = head_blocks(k_ref[s, pl.ds(at, patches), :], head)
                scores.append(dot_nt(q[c * crow : (c + 1) * crow], kbd))
            raised = jnp.exp(jnp.concatenate(scores, axis=0) * scale)
            prob = raised / head_sum(raised, ones)
            p_out[s] = prob
            half = prob.astype(BF16)
            mixed = []
            for c in range(NB):
                img = chunk_img[step * NB + c]
                at = pl.multiple_of(img * patches, patches)
                vbd = head_blocks(v_ref[s, pl.ds(at, patches), :], head)
                mixed.append(dot(half[c * crow : (c + 1) * crow], vbd))
            mixed = jnp.concatenate(mixed, axis=0).astype(BF16)
            attended = attended + dot_nt(mixed, wot_ref[s]).astype(BF16).astype(F32)
        residual = xf + attended
        centred = residual - jnp.mean(residual, axis=-1, keepdims=True)
        variance = jnp.mean(centred * centred, axis=-1, keepdims=True)
        inverse = 1.0 / jnp.sqrt(variance + EPS)
        unit = centred * inverse
        gain = gain_ref[...]
        pooled = jnp.sum((unit * gain).reshape(slots, rows, width), axis=1)
        for j in range(2):
            part = jnp.sum(pooled * itm_ref[j : j + 1], axis=-1, keepdims=True)
            log_out[:, 128 * j : 128 * (j + 1)] = jnp.broadcast_to(part, (slots, 128))
        scaled = (itm_ref[1:2] - itm_ref[0:1]) * gain
        d_first = jnp.mean(scaled, axis=-1, keepdims=True)
        d_second = jnp.mean(scaled * unit, axis=-1, keepdims=True)
        d_out[...] = (inverse * (scaled - d_first - unit * d_second)).astype(BF16)


def backward_kernel(nch, chunk_img, d_ref, p_ref, v_ref, wot_ref, dm_out, ds_out, *, head, scale):
    step = pl.program_id(0)
    shards, _, cols = v_ref.shape
    patches = head
    blocks = (nch[0] + NB - 1) // NB

    @pl.when(step < blocks)
    def _():
        ones = head_ones(cols, head)
        d_res = d_ref[...]
        crow = d_res.shape[0] // NB
        for s in range(shards):
            dm = dot(d_res, wot_ref[s]).astype(BF16)
            dm_out[s] = dm
            d_att = []
            for c in range(NB):
                img = chunk_img[step * NB + c]
                at = pl.multiple_of(img * patches, patches)
                vbd = head_blocks(v_ref[s, pl.ds(at, patches), :], head)
                d_att.append(dot_nt(dm[c * crow : (c + 1) * crow], vbd))
            d_att = jnp.concatenate(d_att, axis=0)
            prob = p_ref[s]
            inner = head_sum(d_att * prob, ones)
            ds_out[s] = prob * (d_att - inner) * scale


def outer_kernel(nch, chunk_img, delta_ref, q_ref, p_ref, dm_ref, ds_ref, out_ref, acc, *, head):
    step = pl.program_id(0)
    cols = q_ref.shape[-1]
    patches = head
    blocks = (nch[0] + NB - 1) // NB

    @pl.when(step == 0)
    def _():
        acc[...] = jnp.zeros_like(acc)

    @pl.when(step < blocks)
    def _():
        delta = delta_ref[:, :1]
        ds = (ds_ref[0] * delta).astype(BF16)
        pd = (p_ref[0] * delta).astype(BF16)
        q = q_ref[0]
        dm = dm_ref[0]
        crow = q.shape[0] // NB
        lane_head = lax.broadcasted_iota(jnp.int32, (patches, cols), 1) // head

        def diagonal(block):
            total = jnp.zeros((patches, cols), F32)
            for h in range(cols // head):
                total = total + jnp.where(
                    lane_head == h, block[h * patches : (h + 1) * patches], 0.0
                )
            return total

        for c in range(NB):
            img = chunk_img[step * NB + c]
            at = pl.multiple_of(img * patches, patches)
            sl = slice(c * crow, (c + 1) * crow)
            dk = diagonal(dot_tn(ds[sl], q[sl]))
            dv = diagonal(dot_tn(pd[sl], dm[sl]))
            acc[pl.ds(at, patches), :] += jnp.concatenate([dk, dv], axis=-1)

    @pl.when(step == pl.num_programs(0) - 1)
    def _():
        out_ref[...] = acc[...].astype(BF16)


def plan(neg_caption, all_images, dp, pair_count, n_slots):
    total = all_images.shape[0]
    index = jnp.arange(pair_count, dtype=jnp.int32)
    own = (all_images // pair_count == dp)[:, None] & (
        (all_images % pair_count)[:, None] == index[None, :]
    )
    order = jnp.arange(total, dtype=jnp.int32)
    below = (order[None, :] <= order[:, None]).astype(BF16)
    upto = dot(below, own.astype(BF16)).astype(jnp.int32)
    count = jnp.sum(own.astype(jnp.int32), axis=0)
    chunks = (2 + count + CE - 1) // CE
    first = jnp.sum(jnp.where(index[None, :] < index[:, None], chunks[None, :], 0), axis=1)
    n_chunks = jnp.sum(chunks)
    slot_of = jnp.sum(jnp.where(own, first[None, :] * CE + 1 + upto, 0), axis=1)
    slot = jnp.arange(n_slots, dtype=jnp.int32)
    img = jnp.sum((slot[:, None] // CE >= first[None, :]).astype(jnp.int32), axis=1) - 1
    at_img = img[:, None] == index[None, :]
    pos = slot - CE * jnp.sum(jnp.where(at_img, first[None, :], 0), axis=1)
    hit = slot[:, None] == slot_of[None, :]
    hit = hit & (pos >= 2)[:, None]
    pushed = jnp.sum(jnp.where(hit, order[None, :], 0), axis=1)
    filled = jnp.any(hit, axis=1)
    negative = jnp.sum(jnp.where(at_img, neg_caption[None, :], 0), axis=1)
    cap = jnp.where(pos == 1, negative, jnp.where(filled, pushed, dp * pair_count + img))
    in_use = (slot // CE < n_chunks) & ((pos < 2) | filled)
    sign = jnp.where(in_use, jnp.where(pos == 0, -1.0, 1.0), 0.0).astype(F32)
    chunk_img = img.reshape(-1, CE)[:, 0]
    return n_chunks, chunk_img, cap, sign, first, hit


def local(
    images, query_states, neg_caption, neg_image, cross_query, cross_kv, cross_out, norm_gain,
    itm_weight,
):
    pair_count, patches, vis = images.shape
    queries, width = query_states.shape[1:]
    cols = cross_query.shape[1]
    head = width // HEADS
    scale = 1.0 / head**0.5
    groups = lax.axis_size("dp")
    shards = lax.axis_size("mp")
    dp, mp = lax.axis_index("dp"), lax.axis_index("mp")
    core = dp % 2
    rows = queries // shards
    half = width // 2
    pairs = groups * pair_count

    def around(x, by):
        return lax.ppermute(x, "mp", [(i, (i + by) % shards) for i in range(shards)])

    def other_core(x):
        return lax.ppermute(x, "dp", [(i, i ^ 1) for i in range(groups)])

    own_rows = lax.dynamic_slice_in_dim(query_states, mp * rows, rows, 1)
    packed = jnp.concatenate([own_rows[:, :, :half], own_rows[:, :, half:]], axis=1)
    pool = lax.all_gather(packed, "dp", axis=0, tiled=True)
    ids = jnp.zeros((8, 128), jnp.int32).at[0, :pair_count].set(neg_image)
    all_images = lax.all_gather(ids, "dp", axis=0, tiled=True)
    all_images = all_images.reshape(groups, 8, 128)[:, 0, :pair_count].reshape(-1)

    weights = jnp.concatenate(
        [
            jnp.concatenate([cross_kv[0], cross_kv[1]], axis=1),
            jnp.concatenate([cross_query, cross_out.T], axis=1),
        ],
        axis=0,
    )
    tall = weights.shape[0] // 2
    mine = lax.dynamic_slice_in_dim(weights, core * tall, tall, 0)
    shard_list = [weights]
    for s in range(1, shards):
        got = around(mine, shards - s)
        swap = other_core(got)
        shard_list.append(
            jnp.concatenate(
                [jnp.where(core == 0, got, swap), jnp.where(core == 0, swap, got)], axis=0
            )
        )
    flat = images.reshape(pair_count * patches, vis)
    kv = [dot(flat, w[:vis]).astype(BF16) for w in shard_list]
    keys = jnp.stack([x[:, :cols] for x in kv])
    values = jnp.stack([x[:, cols:] for x in kv])
    wq = jnp.stack([w[vis:, :cols] for w in shard_list])
    wot = jnp.stack([w[vis:, cols:] for w in shard_list])

    out_rows = vis // groups
    pad_rows = (out_rows + 1 + 7) // 8 * 8
    feature = lax.broadcasted_iota(jnp.int32, (vis, groups * pad_rows), 0)
    place = lax.broadcasted_iota(jnp.int32, (vis, groups * pad_rows), 1)
    target = jnp.where(
        place % pad_rows < out_rows, place // pad_rows * out_rows + place % pad_rows, -1
    )
    chosen = (feature == target).astype(BF16)
    spread = lax.dot_general(
        chosen, flat, (((0,), (1,)), ((), ())), preferred_element_type=F32
    ).astype(BF16)

    steps = -(-(pair_count * (2 + CE - 1) + 2 * groups) // (CE * NB))
    n_slots = steps * NB * CE
    n_chunks, chunk_img, cap, sign, first, hit = plan(
        neg_caption, all_images, dp, pair_count, n_slots
    )
    nch = n_chunks.reshape(1)
    n_rows = n_slots * rows
    blk = NB * CE * rows

    def last(i, nch):
        return jnp.minimum(i, (nch[0] + NB - 1) // NB - 1)

    def whole(a):
        return pl.BlockSpec(a.shape, lambda *_: (0,) * a.ndim)

    row3 = pl.BlockSpec((shards, blk, cols), lambda i, n, *_: (0, last(i, n), 0))
    row2 = pl.BlockSpec((blk, width), lambda i, n, *_: (last(i, n), 0))
    params = pltpu.CompilerParams(vmem_limit_bytes=56 * 2**20)
    gain = norm_gain.reshape(1, width)
    itm = itm_weight.T / queries
    q_rows, prob, d_res, log_part = pl.pallas_call(
        functools.partial(forward_kernel, head=head, scale=scale),
        grid_spec=pltpu.PrefetchScalarGridSpec(
            num_scalar_prefetch=3,
            grid=(steps,),
            in_specs=[
                pl.BlockSpec(memory_space=pl.ANY),
                whole(keys), whole(values), whole(wq), whole(wot), whole(gain), whole(itm),
            ],
            out_specs=[
                row3, row3, row2,
                pl.BlockSpec((NB * CE, 256), lambda i, n, *_: (last(i, n), 0)),
            ],
            scratch_shapes=[
                pltpu.VMEM((n_slots, 2 * rows, half), BF16),
                pltpu.SemaphoreType.DMA((steps,)),
            ],
        ),
        out_shape=[
            jax.ShapeDtypeStruct((shards, n_rows, cols), BF16),
            jax.ShapeDtypeStruct((shards, n_rows, cols), F32),
            jax.ShapeDtypeStruct((n_rows, width), BF16),
            jax.ShapeDtypeStruct((n_slots, 256), F32),
        ],
        compiler_params=params,
        name="forward",
    )(nch, chunk_img, cap, pool, keys, values, wq, wot, gain, itm)

    part = jnp.stack([log_part[:, 0], log_part[:, 128]])
    part = jnp.where((sign != 0.0)[None, :], part, 0.0)
    terms = [part] + [around(part, shards - s) for s in range(1, shards)]
    logits = jnp.zeros_like(part)
    for m in range(shards):
        for s in range(shards):
            logits = logits + jnp.where((mp + s) % shards == m, terms[s], 0.0)

    d_mixed, d_scores = pl.pallas_call(
        functools.partial(backward_kernel, head=head, scale=scale),
        grid_spec=pltpu.PrefetchScalarGridSpec(
            num_scalar_prefetch=2,
            grid=(steps,),
            in_specs=[row2, row3, whole(values), whole(wot)],
            out_specs=[row3, row3],
        ),
        out_shape=[
            jax.ShapeDtypeStruct((shards, n_rows, cols), BF16),
            jax.ShapeDtypeStruct((shards, n_rows, cols), F32),
        ],
        compiler_params=params,
        name="backward",
    )(nch, chunk_img, d_res, prob, values, wot)

    gap = logits[1] - logits[0]
    delta = sign / (1.0 + jnp.exp(-sign * gap))
    delta = jnp.broadcast_to(jnp.repeat(delta, rows)[:, None], (n_rows, 128))

    def outer(s):
        pick = pl.BlockSpec((1, blk, cols), lambda i, n, *_: (s, last(i, n), 0))
        return pl.pallas_call(
            functools.partial(outer_kernel, head=head),
            grid_spec=pltpu.PrefetchScalarGridSpec(
                num_scalar_prefetch=2,
                grid=(steps,),
                in_specs=[
                    pl.BlockSpec((blk, 128), lambda i, n, *_: (last(i, n), 0)),
                    pick, pick, pick, pick,
                ],
                out_specs=pl.BlockSpec(
                    (pair_count * patches, 2 * cols), lambda *_: (0, 0)
                ),
                scratch_shapes=[pltpu.VMEM((pair_count * patches, 2 * cols), F32)],
            ),
            out_shape=jax.ShapeDtypeStruct((pair_count * patches, 2 * cols), BF16),
            compiler_params=params,
            name="outer",
        )(nch, chunk_img, delta, q_rows, prob, d_mixed, d_scores)

    d_kv = sum(
        around(outer(s), s).astype(F32) for s in range(1, shards)
    ) + outer(0).astype(F32)
    upper = d_kv.astype(BF16)
    grad = dot(spread, upper)

    logit_hi = logits.astype(BF16)
    logit_lo = (logits - logit_hi.astype(F32)).astype(BF16)
    four = jnp.concatenate([logit_hi, logit_lo], axis=0)
    home = lax.dot_general(
        hit.astype(BF16), four, (((0,), (1,)), ((), ())), preferred_element_type=F32
    )
    home = jnp.pad(
        home.reshape(groups, 1, 4 * pair_count),
        ((0, 0), (out_rows, pad_rows - out_rows - 1), (0, 2 * cols - 4 * pair_count)),
    )
    leaving = (grad.reshape(groups, pad_rows, 2 * cols) + home).astype(BF16)
    arrived = lax.all_to_all(leaving, "dp", split_axis=0, concat_axis=0, tiled=True)
    summed = jnp.sum(arrived.astype(F32), axis=0)
    grad_part = jnp.transpose(summed[:out_rows].reshape(out_rows, 2, cols), (1, 0, 2))
    back = summed[out_rows, : 4 * pair_count].reshape(pair_count, 2, 2)
    pushed_logits = back[:, 0] + back[:, 1]
    slot = jnp.arange(n_slots, dtype=jnp.int32)[None, :]
    own_logits = []
    for j in range(2):
        here = (first[:, None] * CE + j == slot)[:, None, :]
        own_logits.append(jnp.sum(jnp.where(here, logits[None], 0.0), axis=-1))
    return (jnp.stack(own_logits + [pushed_logits]), grad_part)


def solution(mesh):
    return jax.shard_map(
        local,
        mesh=mesh,
        in_specs=(
            P("dp", None, None),
            P("dp", None, None),
            P("dp"),
            P("dp"),
            P(None, "mp"),
            P(None, None, "mp"),
            P("mp", None),
            P(),
            P(),
        ),
        out_specs=(P(None, "dp", None), P(None, "dp", "mp")),
        check_vma=False,
    )
```

time: 729 us -> 301 us (0.41)
  waiting for transfers between devices: 523 us -> 59.4 us
  Pallas kernels: 0 us -> 68.3 us
  blocking collectives: 0 us -> 46.8 us
  matrix products: 65 us -> 19.2 us
  local copies, waits for them, and re-layouts: 61.2 us -> 19.1 us
  starting transfers between devices: 36.1 us -> 52.7 us
    all_to_all x4 -> x1, waiting for transfers between devices: 268 us -> 31.4 us  [local(): lax.all_to_all(leaving, 'dp', split_axis=0, concat_axis=0, tiled=True)]
    unnamed x4 -> x1, waiting for transfers between devices: 189 us -> 0.02 us
    pallas_call x0 -> x6, Pallas kernels: none -> 68.3 us  [the longest x4 29.2 us: outer(): pl.pallas_call(functools.partial(outer_kernel, head=head), grid_spec=pltp...]
    psum x1 -> x0, waiting for transfers between devices: 66.2 us -> none  [local(): lax.psum(partial_value.astype(jnp.bfloat16), 'mp').astype(jnp.float32)]
    all_gather x0 -> x1, blocking collectives: none -> 46.8 us  [local(): all_images = lax.all_gather(ids, 'dp', axis=0, tiled=True)]
    dot_general x14 -> x7, matrix products: 65 us -> 19.2 us  [the longest x6 18.7 us: dot(): return jnp.dot(a, b, preferred_element_type=F32)]
    ppermute x0 -> x12, starting transfers between devices: none -> 26.4 us  [the longest x9 25.2 us: around(): lax.ppermute(x, 'mp', [(i, (i + by) % shards) for i in range(shards)])]
    ppermute x0 -> x12, waiting for transfers between devices: none -> 25.9 us  [the longest x9 25.2 us: around(): lax.ppermute(x, 'mp', [(i, (i + by) % shards) for i in range(shards)])]
  transfers between devices with their start and end apart: 7 -> 14, of which waited for: 5 -> 6; matrix products, arithmetic and copies ran while one was open for 5% -> 13% of each run, Pallas kernels for 0% -> 7%
where the time goes in v1:
time: 301 us; the launch traced here: 302 us
  Pallas kernels  68.3 us (23%)
  waiting for transfers between devices  59.4 us (20%)
  starting transfers between devices  52.7 us (18%)
  blocking collectives  46.8 us (16%)
  other arithmetic  21.8 us (7%)
  matrix products  19.2 us (6%)
  local copies, waits for them, and re-layouts  19.1 us (6%)
  between operations  14.6 us (5%)
    all_gather x1, blocking collectives, local(): all_images = lax.all_gather(ids, 'dp', axis=0, tiled=True)  46.8 us
    all_to_all x1, waiting for transfers between devices, local(): lax.all_to_all(leaving, 'dp', split_axis=0, concat_axis=0, tiled=True)  31.4 us
    pallas_call x4, Pallas kernels, outer(): pl.pallas_call(functools.partial(outer_kernel, head=head), grid_spec=pltp...  29.2 us
    all_to_all x1, starting transfers between devices, local(): lax.all_to_all(leaving, 'dp', split_axis=0, concat_axis=0, tiled=True)  26.3 us
    pallas_call x1, Pallas kernels, local(): pl.pallas_call(functools.partial(forward_kernel, head=head, scale=scale),...  26 us
    ppermute x9, waiting for transfers between devices, around(): lax.ppermute(x, 'mp', [(i, (i + by) % shards) for i in range(shards)])  25.2 us
    ppermute x9, starting transfers between devices, around(): lax.ppermute(x, 'mp', [(i, (i + by) % shards) for i in range(shards)])  25.2 us
    dot_general x6, matrix products, dot(): return jnp.dot(a, b, preferred_element_type=F32)  18.7 us
  transfers between devices with their start and end apart: 14, of which 6 were waited for; matrix products, arithmetic and copies ran while one was open for 13% of the time, Pallas kernels for 7%

profile of v1, /device:TPU:2, one launch (start us, length us, event | category | flops | bytes accessed | tf_op | source)
XLA Modules:
  0.0 301.9 jit_solution(7244741240787966958)
XLA Ops:
  9.1 2.1 fusion.76
  11.2 2.2 copy.81
  15.7 1.9 copy.66
  17.6 4.6 %fusion.39 = bf16[1088,384]{1,0:T(8,128)(2,1)} fusion(s32[]{:T(128)S(6)} %select_n.313, bf16[1408,192]{1,0:T(8,128)(2,1)} %bitcast.70, bf16[1408,192]{1,0:T(8,128)(2,1)} %bitcast.72, bf16[768,192]{1,0:T(8,128)(2,1)} %copy.66, bf16[768,192]{1,0:T(8,128)(2,1)S(1)} %bitcast.67), kind=kLoop, calls=%fused_computation.57 | loop fusion | flops 3342336 | bytes 2506756 | tf_op jit(solution)/shard_map/concatenate | solution.py:254
  22.2 3.0 collective-permute-start
  26.8 46.8 %all_gather.6 = s32[512,128]{1,0:T(8,128)S(1)} all-gather(s32[8,128]{1,0:T(8,128)S(1)} %scatter.4), channel_id=1, replica_groups=mesh['dp'=64,'mp'=4] {'dp'}, dimensions={0}, use_global_device_ids=true | all-gather | bytes 266240 | tf_op jit(solution)/shard_map/all_gather | solution.py:251
  79.7 3.1 %fusion.21 = bf16[1024,384]{1,0:T(8,128)(2,1)S(1)} fusion(bf16[1024,1408]{1,0:T(8,128)(2,1)S(1)} %bitcast.65, bf16[1408,192]{1,0:T(8,128)(2,1)} %bitcast.73, bf16[1408,192]{1,0:T(8,128)(2,1)} %bitcast.71), kind=kOutput, calls=%fused_computation.34 | convolution fusion | flops 1109852160 | bytes 4751360 | tf_op jit(solution)/shard_map/dot_general | solution.py:19
  89.2 1.7 fusion.22
  91.2 1.7 fusion.23
  93.1 1.7 fusion.24
  95.8 2.0 pad_maximum_fusion.2
  97.9 2.5 pad_maximum_fusion
  100.4 2.1 all-gather.2.cloned.1.call-done.pool
  102.5 26.0 %forward.1 = (bf16[4,2304,192]{2,1,0:T(8,128)(2,1)}, f32[4,2304,192]{2,1,0:T(8,128)}, bf16[2304,768]{1,0:T(8,128)(2,1)}, f32[288,256]{1,0:T(8,128)}) custom-call(s32[1]{0:T(128)} %bitcast.2.nch, s32[36]{0:T(128)} %slice_reduce_fusion.2.chunk_img, s32[288]{0:T(512)} %select_select_fusion.cap_id, bf16[1024,16,384]{2,1,0:T(8,128)(2,1)} %all-gather.2.cloned.1.call-done.pool, ...), custom_call_target="tpu_custom_call" | custom-call | tf_op jit(solution)/shard_map/forward/pallas_call | solution.py:311
  129.6 2.8 collective-permute-start.6
  133.3 12.4 %collective-permute-start.8 = (f32[2,288]{1,0:T(2,128)S(1)}, f32[2,288]{1,0:T(2,128)S(1)}, u32[]{:S(2)}, u32[]{:S(2)}) collective-permute-start(f32[2,288]{1,0:T(2,128)S(1)} %maximum_select_fusion), channel_id=1, source_target_pairs={{0,1},{1,2},{2,3},{3,0},{4,5},{5,6},{6,7},{7,4},{8,9},{9,10},{10,1... | collective-permute-start | bytes 6920 | tf_op jit(solution)/shard_map/ppermute | solution.py:242
  145.7 13.1 %backward.1 = (bf16[4,2304,192]{2,1,0:T(8,128)(2,1)}, f32[4,2304,192]{2,1,0:T(8,128)}) custom-call(s32[1]{0:T(128)} %bitcast.2.nch, s32[36]{0:T(128)} %slice_reduce_fusion.2.chunk_img, bf16[2304,768]{1,0:T(8,128)(2,1)} %get-tuple-element.23.d_ref, f32[4,2304,192]{2,1,0:T(8,128)} %get-tuple-element.22.p_ref, bf16[4,1024,192]{2,1,0:T(8,128)(2,1)} %get-tuple-element.69.v_ref, ...), custom_call_target="tpu_custom_call" | custom-call | tf_op jit(solution)/shard_map/backward/pallas_call | solution.py:347
  159.1 1.4 broadcast_in_dim.175.delta_ref
  160.5 7.3 %outer.4 = bf16[1024,384]{1,0:T(8,128)(2,1)} custom-call(s32[1]{0:T(128)} %bitcast.2.nch, s32[36]{0:T(128)} %slice_reduce_fusion.2.chunk_img, f32[2304,128]{1,0:T(8,128)} %broadcast_in_dim.175.delta_ref, bf16[4,2304,192]{2,1,0:T(8,128)(2,1)} %get-tuple-element.21.q_ref, f32[4,2304,192]{2,1,0:T(8,128)} %get-tuple-element.22.p_ref, ...), custom_call_target="tpu_custom_call" | custom-call | tf_op jit(solution)/shard_map/outer/pallas_call | solution.py:369
  167.8 7.3 %outer.5 = bf16[1024,384]{1,0:T(8,128)(2,1)} custom-call(s32[1]{0:T(128)} %bitcast.2.nch, s32[36]{0:T(128)} %slice_reduce_fusion.2.chunk_img, f32[2304,128]{1,0:T(8,128)} %broadcast_in_dim.175.delta_ref, bf16[4,2304,192]{2,1,0:T(8,128)(2,1)} %get-tuple-element.21.q_ref, f32[4,2304,192]{2,1,0:T(8,128)} %get-tuple-element.22.p_ref, ...), custom_call_target="tpu_custom_call" | custom-call | tf_op jit(solution)/shard_map/outer/pallas_call | solution.py:369
  175.1 7.3 %outer.6 = bf16[1024,384]{1,0:T(8,128)(2,1)} custom-call(s32[1]{0:T(128)} %bitcast.2.nch, s32[36]{0:T(128)} %slice_reduce_fusion.2.chunk_img, f32[2304,128]{1,0:T(8,128)} %broadcast_in_dim.175.delta_ref, bf16[4,2304,192]{2,1,0:T(8,128)(2,1)} %get-tuple-element.21.q_ref, f32[4,2304,192]{2,1,0:T(8,128)} %get-tuple-element.22.p_ref, ...), custom_call_target="tpu_custom_call" | custom-call | tf_op jit(solution)/shard_map/outer/pallas_call | solution.py:369
  182.4 1.8 collective-permute-start.9
  184.2 2.0 collective-permute-start.10
  187.0 7.3 %outer.7 = bf16[1024,384]{1,0:T(8,128)(2,1)} custom-call(s32[1]{0:T(128)} %bitcast.2.nch, s32[36]{0:T(128)} %slice_reduce_fusion.2.chunk_img, f32[2304,128]{1,0:T(8,128)} %broadcast_in_dim.175.delta_ref, bf16[4,2304,192]{2,1,0:T(8,128)(2,1)} %get-tuple-element.21.q_ref, f32[4,2304,192]{2,1,0:T(8,128)} %get-tuple-element.22.p_ref, ...), custom_call_target="tpu_custom_call" | custom-call | tf_op jit(solution)/shard_map/outer/pallas_call | solution.py:369
  195.0 8.8 %collective-permute-done.9 = bf16[1024,384]{1,0:T(8,128)(2,1)} collective-permute-done((bf16[1024,384]{1,0:T(8,128)(2,1)}, bf16[1024,384]{1,0:T(8,128)(2,1)}, u32[]{:S(2)}, u32[]{:S(2)}) %collective-permute-start.9) | collective-permute-done | bytes 786464 | tf_op jit(solution)/shard_map/ppermute | solution.py:242
  203.8 16.4 %collective-permute-done.10 = bf16[1024,384]{1,0:T(8,128)(2,1)} collective-permute-done((bf16[1024,384]{1,0:T(8,128)(2,1)}, bf16[1024,384]{1,0:T(8,128)(2,1)}, u32[]{:S(2)}, u32[]{:S(2)}) %collective-permute-start.10) | collective-permute-done | bytes 786464 | tf_op jit(solution)/shard_map/ppermute | solution.py:242
  220.2 10.0 %fusion.19 = f32[1536,384]{1,0:T(8,128)} fusion(bf16[1024,1408]{1,0:T(8,128)(2,1)S(1)} %bitcast.66, s32[1536]{0:T(1024)S(1)} %get-tuple-element.72, s32[1536]{0:T(1024)S(1)} %get-tuple-element.75, s32[1536]{0:T(1024)S(1)} %get-tuple-element.73, s32[1536]{0:T(1024)S(1)} %get-tuple-element.74, pred[1536]{0:T(1024)(128)(4,1)S(1)} %get-tuple-element.76, ...), kind=kOutput, calls=%fused_computation.29 | convolution fusion | flops 5659164672 | bytes 8416256 | tf_op jit(solution)/shard_map/dot_general | solution.py:19
  230.2 2.0 fusion.17
  232.3 1.7 copy.73
  234.0 26.3 %all-to-all-start = ((bf16[64,24,384]{2,1,0:T(8,128)(2,1)}), bf16[64,24,384]{2,1,0:T(8,128)(2,1)}, u32[]{:S(2)}, u32[]{:S(2)}) async-start(bf16[64,24,384]{2,1,0:T(8,128)(2,1)} %copy.73), calls=%async_computation | async-start | bytes 2359296 | tf_op jit(solution)/shard_map/all_to_all | solution.py:405
  260.5 31.4 %all-to-all-done = bf16[64,24,384]{2,1,0:T(8,128)(2,1)} async-done(((bf16[64,24,384]{2,1,0:T(8,128)(2,1)}), bf16[64,24,384]{2,1,0:T(8,128)(2,1)}, u32[]{:S(2)}, u32[]{:S(2)}) %all-to-all-start) | async-done | bytes 1179680 | tf_op jit(solution)/shard_map/all_to_all | solution.py:405
  291.9 1.5 convert_reduce_fusion
  (90 shorter events, 25.1 us)
Async XLA Ops:
  7.2 72.5 %copy-start = (bf16[16,64,1408]{2,1,0:T(8,128)(2,1)S(1)}, bf16[16,64,1408]{2,1,0:T(8,128)(2,1)}, u32[]{:S(2)}) copy-start(bf16[16,64,1408]{2,1,0:T(8,128)(2,1)} %param.11) | copy-start | bytes 8650756
  7.2 95.3 %all-gather.2.cloned.1.call-start = ((), (), s32[]{:S(2)}) async-start(), calls=%async_computation.1 | async-start | bytes 12779520 | tf_op jit(solution)/shard_map/all_gather | solution.py:249
  14.6 12.3 %copy-start.5 = (s32[16]{0:T(128)S(1)}, s32[16]{0:T(128)}, u32[]{:S(2)}) copy-start(s32[16]{0:T(128)} %param.14) | copy-start | bytes 196
  15.7 59.1 %copy-start.3 = (f32[768]{0:T(1024)S(1)}, f32[768]{0:T(1024)}, u32[]{:S(2)}) copy-start(f32[768]{0:T(1024)} %param.18) | copy-start | bytes 9220
  15.7 59.7 %copy-start.4 = (s32[16]{0:T(128)S(1)}, s32[16]{0:T(128)}, u32[]{:S(2)}) copy-start(s32[16]{0:T(128)} %param.13) | copy-start | bytes 196
  17.6 60.6 %copy-start.2 = (f32[768,2]{0,1:T(2,128)S(1)}, f32[768,2]{0,1:T(2,128)}, u32[]{:S(2)}) copy-start(f32[768,2]{0,1:T(2,128)} %param.19) | copy-start | bytes 18436
  22.2 56.6 %collective-permute-start = (bf16[1088,384]{1,0:T(8,128)(2,1)}, bf16[1088,384]{1,0:T(8,128)(2,1)}, u32[]{:S(2)}, u32[]{:S(2)}) collective-permute-start(bf16[1088,384]{1,0:T(8,128)(2,1)} %fusion.39), channel_id=1, source_target_pairs={{0,3},{1,0},{2,1},{3,2},{4,7},{5,4},{6,5},{7,6},{8,11},{9,8},{10,9... | collective-permute-start | bytes 2506760 | tf_op jit(solution)/shard_map/ppermute | solution.py:242
  25.2 57.9 %collective-permute-start.2 = (bf16[1088,384]{1,0:T(8,128)(2,1)}, bf16[1088,384]{1,0:T(8,128)(2,1)}, u32[]{:S(2)}, u32[]{:S(2)}) collective-permute-start(bf16[1088,384]{1,0:T(8,128)(2,1)} %fusion.39), channel_id=1, source_target_pairs={{0,2},{1,3},{2,0},{3,1},{4,6},{5,7},{6,4},{7,5},{8,10},{9,11},{10,... | collective-permute-start | bytes 2506760 | tf_op jit(solution)/shard_map/ppermute | solution.py:242
  25.8 57.5 %collective-permute-start.4 = (bf16[1088,384]{1,0:T(8,128)(2,1)}, bf16[1088,384]{1,0:T(8,128)(2,1)}, u32[]{:S(2)}, u32[]{:S(2)}) collective-permute-start(bf16[1088,384]{1,0:T(8,128)(2,1)} %fusion.39), channel_id=1, source_target_pairs={{0,1},{1,2},{2,3},{3,0},{4,5},{5,6},{6,7},{7,4},{8,9},{9,10},{10,1... | collective-permute-start | bytes 2506760 | tf_op jit(solution)/shard_map/ppermute | solution.py:242
  78.8 5.1 %collective-permute-start.1 = (bf16[1088,384]{1,0:T(8,128)(2,1)}, bf16[1088,384]{1,0:T(8,128)(2,1)S(1)}, u32[]{:S(2)}, u32[]{:S(2)}) collective-permute-start(bf16[1088,384]{1,0:T(8,128)(2,1)} %collective-permute-done), channel_id=1, source_target_pairs={{0,4},{4,0},{8,12},{12,8},{16,20},{20,16},{24,28},{28,24},{32,36},... | collective-permute-start | bytes 2506760 | tf_op jit(solution)/shard_map/ppermute | solution.py:245
  83.1 2.8 collective-permute-start.3
  83.4 4.3 %collective-permute-start.5 = (bf16[1088,384]{1,0:T(8,128)(2,1)}, bf16[1088,384]{1,0:T(8,128)(2,1)S(1)}, u32[]{:S(2)}, u32[]{:S(2)}) collective-permute-start(bf16[1088,384]{1,0:T(8,128)(2,1)} %collective-permute-done.4), channel_id=1, source_target_pairs={{0,4},{4,0},{8,12},{12,8},{16,20},{20,16},{24,28},{28,24},{32,36},... | collective-permute-start | bytes 2506760 | tf_op jit(solution)/shard_map/ppermute | solution.py:245
  94.8 1.0 copy-start.1
  129.6 29.1 %collective-permute-start.6 = (f32[2,288]{1,0:T(2,128)S(1)}, f32[2,288]{1,0:T(2,128)S(1)}, u32[]{:S(2)}, u32[]{:S(2)}) collective-permute-start(f32[2,288]{1,0:T(2,128)S(1)} %maximum_select_fusion), channel_id=1, source_target_pairs={{0,3},{1,0},{2,1},{3,2},{4,7},{5,4},{6,5},{7,6},{8,11},{9,8},{10,9... | collective-permute-start | bytes 6920 | tf_op jit(solution)/shard_map/ppermute | solution.py:242
  132.5 26.3 %collective-permute-start.7 = (f32[2,288]{1,0:T(2,128)S(1)}, f32[2,288]{1,0:T(2,128)S(1)}, u32[]{:S(2)}, u32[]{:S(2)}) collective-permute-start(f32[2,288]{1,0:T(2,128)S(1)} %maximum_select_fusion), channel_id=1, source_target_pairs={{0,2},{1,3},{2,0},{3,1},{4,6},{5,7},{6,4},{7,5},{8,10},{9,11},{10,... | collective-permute-start | bytes 6920 | tf_op jit(solution)/shard_map/ppermute | solution.py:242
  133.3 25.5 %collective-permute-start.8 = (f32[2,288]{1,0:T(2,128)S(1)}, f32[2,288]{1,0:T(2,128)S(1)}, u32[]{:S(2)}, u32[]{:S(2)}) collective-permute-start(f32[2,288]{1,0:T(2,128)S(1)} %maximum_select_fusion), channel_id=1, source_target_pairs={{0,1},{1,2},{2,3},{3,0},{4,5},{5,6},{6,7},{7,4},{8,9},{9,10},{10,1... | collective-permute-start | bytes 6920 | tf_op jit(solution)/shard_map/ppermute | solution.py:242
  182.4 21.4 %collective-permute-start.9 = (bf16[1024,384]{1,0:T(8,128)(2,1)}, bf16[1024,384]{1,0:T(8,128)(2,1)}, u32[]{:S(2)}, u32[]{:S(2)}) collective-permute-start(bf16[1024,384]{1,0:T(8,128)(2,1)} %outer.4), channel_id=1, source_target_pairs={{0,1},{1,2},{2,3},{3,0},{4,5},{5,6},{6,7},{7,4},{8,9},{9,10},{10,1... | collective-permute-start | bytes 2359304 | tf_op jit(solution)/shard_map/ppermute | solution.py:242
  184.2 36.0 %collective-permute-start.10 = (bf16[1024,384]{1,0:T(8,128)(2,1)}, bf16[1024,384]{1,0:T(8,128)(2,1)}, u32[]{:S(2)}, u32[]{:S(2)}) collective-permute-start(bf16[1024,384]{1,0:T(8,128)(2,1)} %outer.5), channel_id=1, source_target_pairs={{0,2},{1,3},{2,0},{3,1},{4,6},{5,7},{6,4},{7,5},{8,10},{9,11},{10,... | collective-permute-start | bytes 2359304 | tf_op jit(solution)/shard_map/ppermute | solution.py:242
  186.2 34.0 %collective-permute-start.11 = (bf16[1024,384]{1,0:T(8,128)(2,1)}, bf16[1024,384]{1,0:T(8,128)(2,1)}, u32[]{:S(2)}, u32[]{:S(2)}) collective-permute-start(bf16[1024,384]{1,0:T(8,128)(2,1)} %outer.6), channel_id=1, source_target_pairs={{0,3},{1,0},{2,1},{3,2},{4,7},{5,4},{6,5},{7,6},{8,11},{9,8},{10,9... | collective-permute-start | bytes 2359304 | tf_op jit(solution)/shard_map/ppermute | solution.py:242
  234.0 57.9 %all-to-all-start = ((bf16[64,24,384]{2,1,0:T(8,128)(2,1)}), bf16[64,24,384]{2,1,0:T(8,128)(2,1)}, u32[]{:S(2)}, u32[]{:S(2)}) async-start(bf16[64,24,384]{2,1,0:T(8,128)(2,1)} %copy.73), calls=%async_computation | async-start | bytes 2359296 | tf_op jit(solution)/shard_map/all_to_all | solution.py:405
Sparse Core Ops, SparseCore 0:
  10.8 91.6 all-gather.1
